TPU v7x, 256 devices: a whole 4x4x8 slice. The times are simulated.
256 devices in a mesh: ctx: 128 (over x, y_hi, z, core), section: 2 (over y_lo).
Axes of the slice: x: 4, y: 4 (y_hi: 2, y_lo: 2; y = y_hi * 2 + y_lo), z: 8, core: 2. Of those that a mesh axis runs over, the one named last changes fastest.
Arguments:
- query_rows: bfloat16 [2, 32768, 4096], P('section', 'ctx'), may hold values from -140 to 140
- key_rows: bfloat16 [2, 32768, 512], P('section', 'ctx'), may hold values from -5 to 5
- value_rows: bfloat16 [2, 32768, 512], P('section', 'ctx'), may hold values from -6 to 6
- doc_lengths: int32 [32], replicated, may hold values from 256 to 1536, as said below
- rank_plan: int32 [256], replicated, may hold values from 0 to 127, as said below
- tile_mask: int32 [256, 256], replicated, may hold values from 0 to 1, as said below
Outputs:
- handed: bfloat16 [2, 49152, 4096], P('section', 'ctx')
Inputs may be any that keep to these rules, and one draw needn't show every extreme that they name: `doc_lengths`: the lengths sum to 32768; the first is 256; at least one is exactly 1536. Never falling along the blocks; rank_plan[b] // 2 == b // 4; every rank holds 1 to 3 blocks and some rank exactly 3. `tile_mask`: 1 on the diagonal; off it, an entry [i, j] is 1 only where j < i and blocks i and j hold tokens of one document.
All inputs are finite; a program needn't handle non-finite values.
Results may differ from a plain program's by a relative error of at most 0.0054.
Values may be sent and summed in bfloat16 or wider, within the bound.
A program may use at most 128 MiB of HBM per device.

v0:
```python
import math

import jax
import jax.numpy as jnp
from jax import lax
from jax.experimental import pallas as pl
from jax.experimental.pallas import tpu as pltpu
from jax.sharding import PartitionSpec as P

BLOCK = 128
ROWS = 256
HEADS_KV = 4
GROUP = 8
DIM = 128
WIDTH = HEADS_KV * GROUP * DIM
HEAD_COLS = GROUP * DIM
RING = 8
BAND = 13 * BLOCK
SLOTS = 11
SEG = 4
SEG_COLS = HEAD_COLS // SEG
SWAP = HEADS_KV - 1
STEPS = HEADS_KV * SEG
SENT = SWAP * SEG
FACTOR = DIM**-0.5 * math.log2(math.e)
NEG = -1e30


def attention_kernel(
    q_hbm, k_hbm, v_hbm, lengths_hbm, mask_hbm,
    recv_out, side_out,
    qbuf, kv, outb, bias, marks, lengths,
    q_sem, k_sem, v_sem, mark_sem, length_sem,
    swap_send, swap_recv,
    chain_send, chain_recv,
    hop_send, hop_recv,
    sib_send, sib_recv,
    out_send, out_recv,
    mid_send, mid_recv, keep_sem,
):
    me = lax.axis_index("ctx")
    section = lax.axis_index("section")
    core = lax.rem(me, 2)
    chip = me // 2
    z = lax.rem(chip, RING)
    ring = chip // RING
    rings = lax.axis_size("ctx") // (2 * RING)

    def device(ring_at, z_at, core_at):
        return {"ctx": (ring_at * RING + z_at) * 2 + core_at, "section": section}

    z_next = lax.rem(z + 1, RING)
    z_prev = lax.rem(z + RING - 1, RING)
    sibling = device(ring, z, 1 - core)
    ahead = device(ring, z_next, core)
    behind = device(ring, z_prev, core)
    over = device(lax.rem(ring + 1, rings), z, core)
    under = device(lax.rem(ring + rings - 1, rings), z, core)
    partner = {"ctx": me, "section": 1 - section}

    def slot_of(d, z_at):
        direct = (z_at + RING - d) // RING
        return 7 + d + direct * (2 * (3 - d) + core - 7 - d)

    def remote(src, dst, send, recv, to):
        return pltpu.make_async_remote_copy(
            src_ref=src, dst_ref=dst, send_sem=send, recv_sem=recv,
            device_id=to, device_id_type=pl.DeviceIdType.MESH,
        )

    def load_q(h):
        cols = pl.ds(pl.multiple_of(h * HEAD_COLS, HEAD_COLS), HEAD_COLS)
        return pltpu.make_async_copy(q_hbm.at[:, cols], qbuf[h], q_sem.at[h])

    def load_kv(h):
        cols = pl.ds(pl.multiple_of(h * DIM, DIM), DIM)
        return (
            pltpu.make_async_copy(k_hbm.at[:, cols], kv[h].at[6 + core, 0], k_sem.at[h]),
            pltpu.make_async_copy(v_hbm.at[:, cols], kv[h].at[6 + core, 1], v_sem.at[h]),
        )

    mark_row = chip * 4 // 8 * 8
    load_marks = pltpu.make_async_copy(
        mask_hbm.at[pl.ds(pl.multiple_of(mark_row, 8), 8)], marks, mark_sem
    )

    load_lengths = pltpu.make_async_copy(lengths_hbm, lengths, length_sem)

    def swap_q():
        cols = pl.ds(SWAP * HEAD_COLS, HEAD_COLS)
        return remote(q_hbm.at[:, cols], qbuf[SWAP], swap_send.at[2], swap_recv.at[2], partner)

    def swap_kv():
        cols = pl.ds(SWAP * DIM, DIM)
        return (
            remote(k_hbm.at[:, cols], kv[SWAP].at[6 + core, 0],
                   swap_send.at[0], swap_recv.at[0], partner),
            remote(v_hbm.at[:, cols], kv[SWAP].at[6 + core, 1],
                   swap_send.at[1], swap_recv.at[1], partner),
        )

    def chain(h, d, z_at=z_next):
        return remote(
            kv[h].at[slot_of(d - 1, z)], kv[h].at[slot_of(d, z_at)],
            chain_send.at[h, d - 1], chain_recv.at[h, d - 1], ahead,
        )

    def chain_wait(h, d):
        chain(h, d, z).wait_recv()

    def cross(h):
        return remote(kv[h].at[10], kv[h].at[core],
                      hop_send.at[h, 0], hop_recv.at[h, 0], over)

    def back_a(h):
        return remote(kv[h].at[core], kv[h].at[2 + core],
                      hop_send.at[h, 1], hop_recv.at[h, 1], behind)

    def back_b(h):
        return remote(kv[h].at[2 + core], kv[h].at[4 + core],
                      hop_send.at[h, 2], hop_recv.at[h, 2], behind)

    def sib(h, d, core_at=core):
        return remote(kv[h].at[(3 - d) * 2 + core], kv[h].at[(3 - d) * 2 + core_at],
                      sib_send.at[h, d], sib_recv.at[h, d], sibling)

    def sib_wait(h, d):
        sib(h, d, 1 - core).wait_recv()

    def out(i):
        return remote(outb.at[i], recv_out.at[i], out_send.at[i], out_recv.at[i], partner)

    def keep(i):
        return pltpu.make_async_copy(outb.at[i], recv_out.at[i], keep_sem.at[i - SENT])

    middle = pl.ds(pl.multiple_of((1 - core) * BLOCK, BLOCK), BLOCK)

    def mid(i, source):
        return remote(source.at[i, middle], side_out.at[i],
                      mid_send.at[i], mid_recv.at[i], sibling)

    def own_ready(h):
        if h < SWAP:
            for copy in load_kv(h):
                copy.wait()
        else:
            for copy in swap_kv():
                copy.wait_recv()

    def tick(h):
        if 0 <= h + 1 < HEADS_KV:
            chain_wait(h + 1, 3)

            @pl.when(z < 3)
            def _():
                cross(h + 1).start()

            @pl.when(z >= 3)
            def _():
                sib(h + 1, 3).start()

        if 0 <= h + 2 < HEADS_KV:
            chain_wait(h + 2, 2)
            chain(h + 2, 3).start()

            @pl.when(z >= 2)
            def _():
                sib(h + 2, 2).start()

        if 0 <= h + 3 < HEADS_KV:
            chain_wait(h + 3, 1)
            chain(h + 3, 2).start()

            @pl.when(z >= 1)
            def _():
                sib(h + 3, 1).start()

        if 0 <= h + 4 < HEADS_KV:
            own_ready(h + 4)
            chain(h + 4, 1).start()
            sib(h + 4, 0).start()

    def after_cross(n):
        @pl.when(z < 3)
        def _():
            cross(n).wait_recv()
            sib(n, 3).start()

            @pl.when(z >= 1)
            def _():
                back_a(n).start()

    def after_back_a(n):
        @pl.when(z < 2)
        def _():
            back_a(n).wait_recv()
            sib(n, 2).start()

            @pl.when(z == 1)
            def _():
                back_b(n).start()

    def finish(n):
        @pl.when(z == 0)
        def _():
            back_b(n).wait_recv()
            sib(n, 1).start()

        for d in range(4):
            sib_wait(n, d)

        if n < SWAP:
            load_q(n).wait()
        else:
            swap_q().wait_recv()

    for h in range(SWAP):
        for copy in load_kv(h):
            copy.start()
    load_marks.start()
    load_lengths.start()
    for h in range(SWAP):
        load_q(h).start()

    barrier = pltpu.get_barrier_semaphore()
    others = (sibling, ahead, behind, partner, over, under)
    for other in others:
        pl.semaphore_signal(barrier, inc=1, device_id=other, device_id_type=pl.DeviceIdType.MESH)
    pl.semaphore_wait(barrier, len(others))

    tick(-4)
    for copy in swap_kv():
        copy.start()
    swap_q().start()

    load_marks.wait()
    load_lengths.wait()
    first_query = (chip * 4 + core * 2) * BLOCK
    for blk in range(2):
        query = first_query + blk * BLOCK + lax.broadcasted_iota(jnp.int32, (BLOCK, BLOCK), 0)

        def latest(j, carried):
            begin, best = carried
            best = jnp.where(query >= begin, begin, best)
            return begin + lengths[j], best

        _, begin_of = lax.fori_loop(
            0, lengths.shape[0], latest, (jnp.int32(0), jnp.zeros((BLOCK, BLOCK), jnp.int32))
        )
        for j in range(13):
            key_block = chip * 4 + core * 2 + blk - 12 + j
            mark = marks[chip * 4 - mark_row + core * 2 + blk, jnp.maximum(key_block, 0)]
            key = key_block * BLOCK + lax.broadcasted_iota(jnp.int32, (BLOCK, BLOCK), 1)
            seen = (key <= query) & (key >= begin_of) & (mark > 0)
            bias[blk, :, j * BLOCK:(j + 1) * BLOCK] = jnp.where(seen, 0.0, NEG)

    tick(-3)
    tick(-2)
    tick(-1)
    after_cross(0)
    after_back_a(0)
    finish(0)

    def attend(i, h, seg):
        for blk in range(2):
            at = pl.ds(blk * BLOCK, BLOCK)
            cols = [pl.ds(pl.multiple_of(seg * SEG_COLS + u * DIM, DIM), DIM) for u in range(2)]
            queries = jnp.concatenate([qbuf[h][at, c] for c in cols], 0)
            window = pl.ds(core, 7)
            keys = kv[h][window, 0].reshape(7 * ROWS, DIM)[blk * BLOCK:blk * BLOCK + BAND]
            values = kv[h][window, 1].reshape(7 * ROWS, DIM)[blk * BLOCK:blk * BLOCK + BAND]
            scores = lax.dot_general(
                queries, keys, (((1,), (1,)), ((), ())), preferred_element_type=jnp.float32
            )
            scores = scores.reshape(2, BLOCK, BAND) * FACTOR + bias[blk][None]
            top = jnp.max(scores, axis=-1, keepdims=True)
            weights = jnp.exp2(scores - top)
            total = jnp.sum(weights, axis=-1, keepdims=True)
            mixed = lax.dot_general(
                weights.astype(jnp.bfloat16).reshape(2 * BLOCK, BAND), values,
                (((1,), (0,)), ((), ())), preferred_element_type=jnp.float32,
            )
            mixed = (mixed.reshape(2, BLOCK, DIM) / total).astype(jnp.bfloat16)
            for u in range(2):
                outb[i, at, u * DIM:(u + 1) * DIM] = mixed[u]

    for h in range(HEADS_KV):

        def step(seg, _):
            i = h * SEG + seg
            attend(i, h, seg)
            if h < SWAP:
                out(i).start()
            else:
                keep(i).start()
                mid(i, outb).start()

            if h + 1 < HEADS_KV:

                @pl.when(seg == 0)
                def _():
                    tick(h)

                @pl.when(seg == 1)
                def _():
                    after_cross(h + 1)

                @pl.when(seg == 2)
                def _():
                    after_back_a(h + 1)

                @pl.when(seg == 3)
                def _():
                    finish(h + 1)

            return 0

        lax.fori_loop(0, SEG, step, 0)

    def pass_on(i, _):
        out(i).wait_recv()
        mid(i, recv_out).start()
        return 0

    lax.fori_loop(0, SENT, pass_on, 0)

    for copy in swap_kv():
        copy.wait_send()
    swap_q().wait_send()

    for h in range(HEADS_KV):
        for d in range(3):
            chain(h, d + 1).wait_send()
        for d in range(4):
            sib(h, d).wait_send()

        @pl.when(z < 3)
        def _():
            cross(h).wait_send()

        @pl.when((z == 1) | (z == 2))
        def _():
            back_a(h).wait_send()

        @pl.when(z == 1)
        def _():
            back_b(h).wait_send()

    def drain_kept(i, _):
        keep(i).wait()
        mid(i, outb).wait()
        return 0

    lax.fori_loop(SENT, STEPS, drain_kept, 0)

    def drain_sent(i, _):
        out(i).wait_send()
        mid(i, recv_out).wait()
        return 0

    lax.fori_loop(0, SENT, drain_sent, 0)


def place_kernel(plan, own, side, placed, zeros, sems):
    me = lax.axis_index("ctx")
    core = lax.rem(me, 2)
    first = me // 2 * 4
    count = jnp.int32(0)
    for j in range(4):
        count += (plan[first + j] == me).astype(jnp.int32)
    zeros[...] = jnp.zeros_like(zeros)
    skip = jnp.where(core == 0, 0, 3 - count)

    def each(i, _):
        cols = pl.ds(pl.multiple_of(i * SEG_COLS, SEG_COLS), SEG_COLS)
        for j in range(3):
            to = placed.at[pl.ds(j * BLOCK, BLOCK), cols]
            at = j + skip
            own_at = jnp.where(core == 0, at, at - 1)
            is_side = at == jnp.where(core == 0, 2, 0)
            own_rows = pl.ds(pl.multiple_of(jnp.clip(own_at, 0, 1) * BLOCK, BLOCK), BLOCK)
            fill = pltpu.make_async_copy(zeros, to, sems.at[i, j])
            from_side = pltpu.make_async_copy(side.at[i], to, sems.at[i, j])
            from_own = pltpu.make_async_copy(own.at[i, own_rows], to, sems.at[i, j])
            pl.when(j >= count)(fill.start)
            pl.when((j < count) & is_side)(from_side.start)
            pl.when((j < count) & jnp.logical_not(is_side))(from_own.start)
        return 0

    lax.fori_loop(0, STEPS, each, 0)

    def finish(i, _):
        cols = pl.ds(pl.multiple_of(i * SEG_COLS, SEG_COLS), SEG_COLS)
        for j in range(3):
            to = placed.at[pl.ds(j * BLOCK, BLOCK), cols]
            pltpu.make_async_copy(zeros, to, sems.at[i, j]).wait()
        return 0

    lax.fori_loop(0, STEPS, finish, 0)


def body(query_rows, key_rows, value_rows, doc_lengths, rank_plan, tile_mask):
    dma = pltpu.SemaphoreType.DMA
    anywhere = pl.BlockSpec(memory_space=pl.ANY)
    held = pl.BlockSpec(memory_space=pltpu.HBM)
    scalars = pl.BlockSpec(memory_space=pltpu.SMEM)
    pinned = [
        pltpu.with_memory_space_constraint(x, pltpu.HBM)
        for x in (query_rows[0], key_rows[0], value_rows[0], doc_lengths, tile_mask)
    ]
    received, side = pl.pallas_call(
        attention_kernel,
        out_shape=(
            jax.ShapeDtypeStruct((STEPS, ROWS, SEG_COLS), jnp.bfloat16),
            jax.ShapeDtypeStruct((STEPS, BLOCK, SEG_COLS), jnp.bfloat16),
        ),
        in_specs=[held] * 5,
        out_specs=(anywhere, anywhere),
        scratch_shapes=[
            [pltpu.VMEM((ROWS, HEAD_COLS), jnp.bfloat16)] * HEADS_KV,
            [pltpu.VMEM((SLOTS, 2, ROWS, DIM), jnp.bfloat16)] * HEADS_KV,
            pltpu.VMEM((STEPS, ROWS, SEG_COLS), jnp.bfloat16),
            pltpu.VMEM((2, BLOCK, BAND), jnp.float32),
            pltpu.SMEM((8, tile_mask.shape[1]), jnp.int32),
            pltpu.SMEM(doc_lengths.shape, jnp.int32),
            dma((SWAP,)), dma((SWAP,)), dma((SWAP,)), dma, dma,
            dma((3,)), dma((3,)),
            dma((HEADS_KV, 3)), dma((HEADS_KV, 3)),
            dma((HEADS_KV, 3)), dma((HEADS_KV, 3)),
            dma((HEADS_KV, 4)), dma((HEADS_KV, 4)),
            dma((SENT,)), dma((SENT,)),
            dma((STEPS,)), dma((STEPS,)), dma((STEPS - SENT,)),
        ],
        compiler_params=pltpu.CompilerParams(
            collective_id=0, has_side_effects=True, vmem_limit_bytes=48 * 1024 * 1024
        ),
        name="attention",
    )(*pinned)
    placed = pl.pallas_call(
        place_kernel,
        out_shape=jax.ShapeDtypeStruct((3 * BLOCK, WIDTH), jnp.bfloat16),
        in_specs=[scalars, anywhere, anywhere],
        out_specs=held,
        compiler_params=pltpu.CompilerParams(vmem_limit_bytes=8 * 1024 * 1024),
        scratch_shapes=[pltpu.VMEM((BLOCK, SEG_COLS), jnp.bfloat16), dma((STEPS, 3))],
        name="place",
    )(rank_plan, received, side)
    return placed[None]


def solution(mesh):
    placed = (
        P("section", "ctx", None),
        P("section", "ctx", None),
        P("section", "ctx", None),
        P(),
        P(),
        P(),
    )
    return jax.shard_map(
        body, mesh=mesh, in_specs=placed, out_specs=P("section", "ctx", None), check_vma=False
    )
```

profile of v0, /device:TPU:1, one launch (start us, length us, event | category | flops | bytes accessed | tf_op | source)
XLA Modules:
  0.0 95.3 jit_solution(14536617473055374683)
XLA Ops:
  0.0 0.0 copy-start
  0.0 92.7 %attention.1 = (bf16[16,256,256]{2,1,0:T(8,128)(2,1)S(1)}, bf16[16,128,256]{2,1,0:T(8,128)(2,1)S(1)}) custom-call(bf16[256,4096]{1,0:T(8,128)(2,1)} %bitcast.4, bf16[256,512]{1,0:T(8,128)(2,1)} %bitcast.5, bf16[256,512]{1,0:T(8,128)(2,1)} %bitcast.6, s32[32]{0:T(128)} %lengths_hbm.1, s32[256,256]{1,0:T(8,128)} %mask_hbm.1), custom_call_target="tpu_custom_call" | custom-call | tf_op jit(solution)/shard_map/attention/pallas_call | solution.py:411
  92.7 0.0 copy-done
  92.7 2.6 %place.1 = bf16[384,4096]{1,0:T(8,128)(2,1)} custom-call(s32[256]{0:T(256)S(1)} %copy-done, bf16[16,256,256]{2,1,0:T(8,128)(2,1)S(1)} %get-tuple-element.7.own, bf16[16,128,256]{2,1,0:T(8,128)(2,1)S(1)} %get-tuple-element.8.side), custom_call_target="tpu_custom_call" | custom-call | tf_op jit(solution)/shard_map/place/pallas_call | solution.py:439
Async XLA Ops:
  0.0 92.7 %copy-start = (s32[256]{0:T(256)S(1)}, s32[256]{0:T(256)}, u32[]{:S(2)}) copy-start(s32[256]{0:T(256)} %plan.1) | copy-start | bytes 3076
where the time goes:
time: 95.4 us; the launch traced here: 95.3 us
  Pallas kernels  95.3 us (100%)
    pallas_call x1, Pallas kernels, body(): pl.pallas_call(attention_kernel, out_shape=(jax.ShapeDtypeStruct((STEPS,...  92.7 us
    pallas_call x1, Pallas kernels, body(): pl.pallas_call(place_kernel, out_shape=jax.ShapeDtypeStruct((3 * BLOCK, W...  2.63 us

commit v1 on v0

--- a/solution.py
+++ b/solution.py
@@ -16,7 +16,8 @@
 HEAD_COLS = GROUP * DIM
 RING = 8
 BAND = 13 * BLOCK
-SLOTS = 11
+PART = 4 * BLOCK
+SLOTS = 10
 SEG = 4
 SEG_COLS = HEAD_COLS // SEG
 SWAP = HEADS_KV - 1
@@ -33,7 +34,7 @@
     q_sem, k_sem, v_sem, mark_sem, length_sem,
     swap_send, swap_recv,
     chain_send, chain_recv,
-    hop_send, hop_recv,
+    hop_send, hop_recv, cross_send, cross_recv,
     sib_send, sib_recv,
     out_send, out_recv,
     mid_send, mid_recv, keep_sem,
@@ -58,9 +59,8 @@
     under = device(lax.rem(ring + rings - 1, rings), z, core)
     partner = {"ctx": me, "section": 1 - section}
 
-    def slot_of(d, z_at):
-        direct = (z_at + RING - d) // RING
-        return 7 + d + direct * (2 * (3 - d) + core - 7 - d)
+    def held(d):
+        return (3 - d) * 2 + core
 
     def remote(src, dst, send, recv, to):
         return pltpu.make_async_remote_copy(
@@ -86,9 +86,11 @@
 
     load_lengths = pltpu.make_async_copy(lengths_hbm, lengths, length_sem)
 
-    def swap_q():
-        cols = pl.ds(SWAP * HEAD_COLS, HEAD_COLS)
-        return remote(q_hbm.at[:, cols], qbuf[SWAP], swap_send.at[2], swap_recv.at[2], partner)
+    def swap_q(seg):
+        cols = pl.ds(SWAP * HEAD_COLS + seg * SEG_COLS, SEG_COLS)
+        to = pl.ds(seg * SEG_COLS, SEG_COLS)
+        return remote(q_hbm.at[:, cols], qbuf[SWAP].at[:, to],
+                      swap_send.at[2 + seg], swap_recv.at[2 + seg], partner)
 
     def swap_kv():
         cols = pl.ds(SWAP * DIM, DIM)
@@ -99,26 +101,23 @@
                    swap_send.at[1], swap_recv.at[1], partner),
         )
 
-    def chain(h, d, z_at=z_next):
-        return remote(
-            kv[h].at[slot_of(d - 1, z)], kv[h].at[slot_of(d, z_at)],
-            chain_send.at[h, d - 1], chain_recv.at[h, d - 1], ahead,
-        )
-
-    def chain_wait(h, d):
-        chain(h, d, z).wait_recv()
+    def chain(h, d):
+        return remote(kv[h].at[held(d - 1)], kv[h].at[held(d)],
+                      chain_send.at[h, d - 1], chain_recv.at[h, d - 1], ahead)
 
     def cross(h):
-        return remote(kv[h].at[10], kv[h].at[core],
-                      hop_send.at[h, 0], hop_recv.at[h, 0], over)
-
-    def back_a(h):
-        return remote(kv[h].at[core], kv[h].at[2 + core],
-                      hop_send.at[h, 1], hop_recv.at[h, 1], behind)
-
-    def back_b(h):
-        return remote(kv[h].at[2 + core], kv[h].at[4 + core],
-                      hop_send.at[h, 2], hop_recv.at[h, 2], behind)
+        return remote(kv[h].at[6 + core], kv[h].at[8], cross_send.at[h], cross_recv.at[h], over)
+
+    def wrap(h):
+        return remote(kv[h].at[8], kv[h].at[held(1)], chain_send.at[h, 0], chain_recv.at[h, 0], ahead)
+
+    def stride_one(h):
+        return remote(kv[h].at[8], kv[h].at[9], hop_send.at[h, 0], hop_recv.at[h, 0],
+                      device(ring, lax.rem(z + RING - 3, RING), core))
+
+    def stride_two(h, d):
+        return remote(kv[h].at[9], kv[h].at[held(d)], hop_send.at[h, d - 1], hop_recv.at[h, d - 1],
+                      device(ring, 0, core))
 
     def sib(h, d, core_at=core):
         return remote(kv[h].at[(3 - d) * 2 + core], kv[h].at[(3 - d) * 2 + core_at],
@@ -147,72 +146,75 @@
             for copy in swap_kv():
                 copy.wait_recv()
 
+    def at_z(place, *actions):
+        @pl.when(z == place)
+        def _():
+            for action in actions:
+                action()
+
+    def ready(n, e):
+        if e < 3:
+
+            @pl.when(z < RING - 1)
+            def _():
+                chain(n, e + 1).start()
+
+        sib(n, e).start()
+
+    def arrive(n, d):
+        chain(n, d).wait_recv()
+        ready(n, d)
+
+    def arrive_over(n, d):
+        if d == 1:
+            chain(n, d).wait_recv()
+        else:
+            at_z(0, stride_two(n, d).wait_recv)
+            pl.when(z > 0)(chain(n, d).wait_recv)
+        ready(n, d)
+
+    def own(n):
+        own_ready(n)
+
+        @pl.when(z >= RING - 3)
+        def _():
+            cross(n).start()
+
     def tick(h):
-        if 0 <= h + 1 < HEADS_KV:
-            chain_wait(h + 1, 3)
-
-            @pl.when(z < 3)
-            def _():
-                cross(h + 1).start()
-
-            @pl.when(z >= 3)
-            def _():
-                sib(h + 1, 3).start()
-
-        if 0 <= h + 2 < HEADS_KV:
-            chain_wait(h + 2, 2)
-            chain(h + 2, 3).start()
-
-            @pl.when(z >= 2)
-            def _():
-                sib(h + 2, 2).start()
-
-        if 0 <= h + 3 < HEADS_KV:
-            chain_wait(h + 3, 1)
-            chain(h + 3, 2).start()
-
-            @pl.when(z >= 1)
-            def _():
-                sib(h + 3, 1).start()
-
-        if 0 <= h + 4 < HEADS_KV:
-            own_ready(h + 4)
-            chain(h + 4, 1).start()
-            sib(h + 4, 0).start()
-
-    def after_cross(n):
-        @pl.when(z < 3)
-        def _():
-            cross(n).wait_recv()
-            sib(n, 3).start()
-
-            @pl.when(z >= 1)
-            def _():
-                back_a(n).start()
-
-    def after_back_a(n):
-        @pl.when(z < 2)
-        def _():
-            back_a(n).wait_recv()
-            sib(n, 2).start()
-
-            @pl.when(z == 1)
-            def _():
-                back_b(n).start()
+        now = h + 4
+        for n in range(HEADS_KV):
+            if now == n == 0:
+                own(n)
+        for d in (3, 2, 1):
+            if 0 <= now - d - 1 < HEADS_KV:
+                pl.when(z < d)(lambda: arrive_over(now - d - 1, d))
+            if 0 <= now - d < HEADS_KV:
+                pl.when(z >= d)(lambda: arrive(now - d, d))
+        if now < HEADS_KV:
+            ready(now, 0)
+        if now + 1 < HEADS_KV:
+            own(now + 1)
+        for n in range(HEADS_KV):
+            if now == max(2, n + 1):
+                at_z(3, stride_one(n).wait_recv, stride_two(n, 2).start)
+                at_z(2, stride_one(n).wait_recv, stride_two(n, 3).start)
+            if now == max(1, n):
+                at_z(RING - 1, cross(n).wait_recv, wrap(n).start)
+
+                @pl.when((z == RING - 2) | (z == RING - 3))
+                def _():
+                    cross(n).wait_recv()
+                    stride_one(n).start()
 
     def finish(n):
-        @pl.when(z == 0)
-        def _():
-            back_b(n).wait_recv()
-            sib(n, 1).start()
-
         for d in range(4):
             sib_wait(n, d)
 
         if n < SWAP:
             load_q(n).wait()
         else:
-            swap_q().wait_recv()
+            for seg in range(SEG):
+                swap_q(seg).wait_recv()
 
     for h in range(SWAP):
         for copy in load_kv(h):
@@ -223,15 +225,29 @@
         load_q(h).start()
 
     barrier = pltpu.get_barrier_semaphore()
-    others = (sibling, ahead, behind, partner, over, under)
-    for other in others:
+    def greet(other):
         pl.semaphore_signal(barrier, inc=1, device_id=other, device_id_type=pl.DeviceIdType.MESH)
-    pl.semaphore_wait(barrier, len(others))
+
+    for other in (sibling, ahead, behind, partner):
+        greet(other)
+    pairs = ((5, 2), (6, 3), (3, 0), (2, 0))
+    for a, b in pairs:
+        at_z(a, lambda: greet(device(ring, b, core)))
+        at_z(b, lambda: greet(device(ring, a, core)))
+
+    @pl.when(z >= RING - 3)
+    def _():
+        greet(over)
+        greet(under)
+
+    for place in range(RING):
+        greeted = 4 + 2 * (place >= RING - 3) + sum(pair.count(place) for pair in pairs)
+        at_z(place, lambda: pl.semaphore_wait(barrier, greeted))
 
     tick(-4)
     for copy in swap_kv():
         copy.start()
-    swap_q().start()
+    swap_q(0).start()
 
     load_marks.wait()
     load_lengths.wait()
@@ -254,11 +270,17 @@
             seen = (key <= query) & (key >= begin_of) & (mark > 0)
             bias[blk, :, j * BLOCK:(j + 1) * BLOCK] = jnp.where(seen, 0.0, NEG)
 
-    tick(-3)
-    tick(-2)
-    tick(-1)
-    after_cross(0)
-    after_back_a(0)
+    for h in (-3, -2, -1):
+        tick(h)
+        swap_q(h + 4).start()
+
+    def early_tick(h):
+        pl.when(z < 3)(lambda: tick(h))
+
+    def late_tick(h):
+        pl.when(z >= 3)(lambda: tick(h))
+
+    early_tick(0)
     finish(0)
 
     def attend(i, h, seg):
@@ -269,20 +291,34 @@
             window = pl.ds(core, 7)
             keys = kv[h][window, 0].reshape(7 * ROWS, DIM)[blk * BLOCK:blk * BLOCK + BAND]
             values = kv[h][window, 1].reshape(7 * ROWS, DIM)[blk * BLOCK:blk * BLOCK + BAND]
-            scores = lax.dot_general(
-                queries, keys, (((1,), (1,)), ((), ())), preferred_element_type=jnp.float32
-            )
-            scores = scores.reshape(2, BLOCK, BAND) * FACTOR + bias[blk][None]
-            top = jnp.max(scores, axis=-1, keepdims=True)
-            weights = jnp.exp2(scores - top)
-            total = jnp.sum(weights, axis=-1, keepdims=True)
-            mixed = lax.dot_general(
-                weights.astype(jnp.bfloat16).reshape(2 * BLOCK, BAND), values,
-                (((1,), (0,)), ((), ())), preferred_element_type=jnp.float32,
-            )
-            mixed = (mixed.reshape(2, BLOCK, DIM) / total).astype(jnp.bfloat16)
+            parts = []
+            top = None
+            for first in range(0, BAND, PART):
+                cut = slice(first, min(first + PART, BAND))
+                scores = lax.dot_general(
+                    queries, keys[cut], (((1,), (1,)), ((), ())), preferred_element_type=jnp.float32
+                )
+                scores = scores.reshape(2, BLOCK, -1) * FACTOR + bias[blk, :, cut][None]
+                parts.append((cut, scores))
+                highest = jnp.max(scores, axis=-1, keepdims=True)
+                top = highest if top is None else jnp.maximum(top, highest)
+            mixed = jnp.zeros((2 * BLOCK, 2 * DIM), jnp.float32)
+            for cut, scores in parts:
+                weights = jnp.exp2(scores - top).astype(jnp.bfloat16).reshape(2 * BLOCK, -1)
+                summed = jnp.concatenate([values[cut], jnp.ones_like(values[cut])], 1)
+                mixed += lax.dot_general(
+                    weights, summed, (((1,), (0,)), ((), ())), preferred_element_type=jnp.float32
+                )
+            mixed = (mixed[:, :DIM] / mixed[:, DIM:]).astype(jnp.bfloat16).reshape(2, BLOCK, DIM)
             for u in range(2):
                 outb[i, at, u * DIM:(u + 1) * DIM] = mixed[u]
+
+    services = (
+        ((), (lambda: late_tick(0),), (), (lambda: early_tick(1), lambda: finish(1))),
+        ((lambda: late_tick(1),), (), (), (lambda: early_tick(2), lambda: finish(2))),
+        ((lambda: late_tick(2),), (), (), (lambda: early_tick(3), lambda: finish(3))),
+        ((), (), (), ()),
+    )
 
     for h in range(HEADS_KV):
 
@@ -295,23 +331,13 @@
                 keep(i).start()
                 mid(i, outb).start()
 
-            if h + 1 < HEADS_KV:
-
-                @pl.when(seg == 0)
-                def _():
-                    tick(h)
-
-                @pl.when(seg == 1)
-                def _():
-                    after_cross(h + 1)
-
-                @pl.when(seg == 2)
-                def _():
-                    after_back_a(h + 1)
-
-                @pl.when(seg == 3)
-                def _():
-                    finish(h + 1)
+            for at in range(SEG):
+                if services[h][at]:
+
+                    @pl.when(seg == at)
+                    def _():
+                        for service in services[h][at]:
+                            service()
 
             return 0
 
@@ -326,25 +352,19 @@
 
     for copy in swap_kv():
         copy.wait_send()
-    swap_q().wait_send()
+    for seg in range(SEG):
+        swap_q(seg).wait_send()
 
     for h in range(HEADS_KV):
-        for d in range(3):
-            chain(h, d + 1).wait_send()
+        for d in (1, 2, 3):
+            pl.when(z < RING - 1)(chain(h, d).wait_send)
+        pl.when(z >= RING - 3)(cross(h).wait_send)
+        at_z(RING - 1, wrap(h).wait_send)
+        pl.when((z == RING - 2) | (z == RING - 3))(stride_one(h).wait_send)
+        at_z(3, stride_two(h, 2).wait_send)
+        at_z(2, stride_two(h, 3).wait_send)
         for d in range(4):
             sib(h, d).wait_send()
-
-        @pl.when(z < 3)
-        def _():
-            cross(h).wait_send()
-
-        @pl.when((z == 1) | (z == 2))
-        def _():
-            back_a(h).wait_send()
-
-        @pl.when(z == 1)
-        def _():
-            back_b(h).wait_send()
 
     def drain_kept(i, _):
         keep(i).wait()
@@ -424,9 +444,9 @@
             pltpu.SMEM((8, tile_mask.shape[1]), jnp.int32),
             pltpu.SMEM(doc_lengths.shape, jnp.int32),
             dma((SWAP,)), dma((SWAP,)), dma((SWAP,)), dma, dma,
-            dma((3,)), dma((3,)),
+            dma((2 + SEG,)), dma((2 + SEG,)),
             dma((HEADS_KV, 3)), dma((HEADS_KV, 3)),
-            dma((HEADS_KV, 3)), dma((HEADS_KV, 3)),
+            dma((HEADS_KV, 3)), dma((HEADS_KV, 3)), dma((HEADS_KV,)), dma((HEADS_KV,)),
             dma((HEADS_KV, 4)), dma((HEADS_KV, 4)),
             dma((SENT,)), dma((SENT,)),
             dma((STEPS,)), dma((STEPS,)), dma((STEPS - SENT,)),

time: 95.4 us -> 81.4 us (0.85)
  Pallas kernels: 95.3 us -> 80.6 us
    pallas_call x1, Pallas kernels: 92.7 us -> 78 us  [body(): pl.pallas_call(attention_kernel, out_shape=(jax.ShapeDtypeStruct((STEPS,...]
where the time goes in v1:
time: 81.4 us; the launch traced here: 80.6 us
  Pallas kernels  80.6 us (99%)
    pallas_call x1, Pallas kernels, body(): pl.pallas_call(attention_kernel, out_shape=(jax.ShapeDtypeStruct((STEPS,...  78 us
    pallas_call x1, Pallas kernels, body(): pl.pallas_call(place_kernel, out_shape=jax.ShapeDtypeStruct((3 * BLOCK, W...  2.63 us

profile of v1, /device:TPU:1, one launch (start us, length us, event | category | flops | bytes accessed | tf_op | source)
XLA Modules:
  0.0 80.6 jit_solution(13320060690474680227)
XLA Ops:
  0.0 0.0 copy-start
  0.0 78.0 %attention.1 = (bf16[16,256,256]{2,1,0:T(8,128)(2,1)S(1)}, bf16[16,128,256]{2,1,0:T(8,128)(2,1)S(1)}) custom-call(bf16[256,4096]{1,0:T(8,128)(2,1)} %bitcast.4, bf16[256,512]{1,0:T(8,128)(2,1)} %bitcast.5, bf16[256,512]{1,0:T(8,128)(2,1)} %bitcast.6, s32[32]{0:T(128)} %lengths_hbm.1, s32[256,256]{1,0:T(8,128)} %mask_hbm.1), custom_call_target="tpu_custom_call" | custom-call | tf_op jit(solution)/shard_map/attention/pallas_call | solution.py:431
  78.0 0.0 copy-done
  78.0 2.6 %place.1 = bf16[384,4096]{1,0:T(8,128)(2,1)} custom-call(s32[256]{0:T(256)S(1)} %copy-done, bf16[16,256,256]{2,1,0:T(8,128)(2,1)S(1)} %get-tuple-element.7.own, bf16[16,128,256]{2,1,0:T(8,128)(2,1)S(1)} %get-tuple-element.8.side), custom_call_target="tpu_custom_call" | custom-call | tf_op jit(solution)/shard_map/place/pallas_call | solution.py:459
Async XLA Ops:
  0.0 78.0 %copy-start = (s32[256]{0:T(256)S(1)}, s32[256]{0:T(256)}, u32[]{:S(2)}) copy-start(s32[256]{0:T(256)} %plan.1) | copy-start | bytes 3076

commit v2 on v1

--- a/solution.py
+++ b/solution.py
@@ -186,7 +186,7 @@
             if now == n == 0:
                 own(n)
         for d in (3, 2, 1):
-            if 0 <= now - d - 1 < HEADS_KV:
+            if 0 <= now - d - 1 < HEADS_KV and (now, d) != (4, 3):
                 pl.when(z < d)(lambda: arrive_over(now - d - 1, d))
             if 0 <= now - d < HEADS_KV:
                 pl.when(z >= d)(lambda: arrive(now - d, d))
@@ -280,7 +280,7 @@
     def late_tick(h):
         pl.when(z >= 3)(lambda: tick(h))
 
-    early_tick(0)
+    pl.when(z < 3)(lambda: arrive_over(0, 3))
     finish(0)
 
     def attend(i, h, seg):
@@ -314,7 +314,7 @@
                 outb[i, at, u * DIM:(u + 1) * DIM] = mixed[u]
 
     services = (
-        ((), (lambda: late_tick(0),), (), (lambda: early_tick(1), lambda: finish(1))),
+        ((lambda: early_tick(0),), (lambda: late_tick(0),), (), (lambda: early_tick(1), lambda: finish(1))),
         ((lambda: late_tick(1),), (), (), (lambda: early_tick(2), lambda: finish(2))),
         ((lambda: late_tick(2),), (), (), (lambda: early_tick(3), lambda: finish(3))),
         ((), (), (), ()),

time: 81.4 us -> 80.7 us (level)
  no operation moved by 1% of the time
where the time goes in v2:
time: 80.7 us; the launch traced here: 80.6 us
  Pallas kernels  80.6 us (100%)
    pallas_call x1, Pallas kernels, body(): pl.pallas_call(attention_kernel, out_shape=(jax.ShapeDtypeStruct((STEPS,...  78 us
    pallas_call x1, Pallas kernels, body(): pl.pallas_call(place_kernel, out_shape=jax.ShapeDtypeStruct((3 * BLOCK, W...  2.63 us

profile of v2, /device:TPU:1, one launch (start us, length us, event | category | flops | bytes accessed | tf_op | source)
XLA Modules:
  0.0 80.6 jit_solution(11240489310023539477)
XLA Ops:
  0.0 0.0 copy-start
  0.0 78.0 %attention.1 = (bf16[16,256,256]{2,1,0:T(8,128)(2,1)S(1)}, bf16[16,128,256]{2,1,0:T(8,128)(2,1)S(1)}) custom-call(bf16[256,4096]{1,0:T(8,128)(2,1)} %bitcast.4, bf16[256,512]{1,0:T(8,128)(2,1)} %bitcast.5, bf16[256,512]{1,0:T(8,128)(2,1)} %bitcast.6, s32[32]{0:T(128)} %lengths_hbm.1, s32[256,256]{1,0:T(8,128)} %mask_hbm.1), custom_call_target="tpu_custom_call" | custom-call | tf_op jit(solution)/shard_map/attention/pallas_call | solution.py:431
  78.0 0.0 copy-done
  78.0 2.6 %place.1 = bf16[384,4096]{1,0:T(8,128)(2,1)} custom-call(s32[256]{0:T(256)S(1)} %copy-done, bf16[16,256,256]{2,1,0:T(8,128)(2,1)S(1)} %get-tuple-element.7.own, bf16[16,128,256]{2,1,0:T(8,128)(2,1)S(1)} %get-tuple-element.8.side), custom_call_target="tpu_custom_call" | custom-call | tf_op jit(solution)/shard_map/place/pallas_call | solution.py:459
Async XLA Ops:
  0.0 78.0 %copy-start = (s32[256]{0:T(256)S(1)}, s32[256]{0:T(256)}, u32[]{:S(2)}) copy-start(s32[256]{0:T(256)} %plan.1) | copy-start | bytes 3076

commit v3 on v2

--- a/solution.py
+++ b/solution.py
@@ -195,10 +195,10 @@
         if now + 1 < HEADS_KV:
             own(now + 1)
         for n in range(HEADS_KV):
-            if now == max(2, n + 1):
+            if now == n + 2:
                 at_z(3, stride_one(n).wait_recv, stride_two(n, 2).start)
                 at_z(2, stride_one(n).wait_recv, stride_two(n, 3).start)
-            if now == max(1, n):
+            if now == n + 1:
                 at_z(RING - 1, cross(n).wait_recv, wrap(n).start)
 
                 @pl.when((z == RING - 2) | (z == RING - 3))

time: 80.7 us -> 76.8 us (0.952)
  the two profiles are of different devices: /device:TPU:1 before, /device:TPU:41 now
where the time goes in v3:
time: 76.8 us; the launch traced here: 76.7 us
  Pallas kernels  76.7 us (100%)
    pallas_call x1, Pallas kernels, body(): pl.pallas_call(attention_kernel, out_shape=(jax.ShapeDtypeStruct((STEPS,...  74.1 us
    pallas_call x1, Pallas kernels, body(): pl.pallas_call(place_kernel, out_shape=jax.ShapeDtypeStruct((3 * BLOCK, W...  2.63 us

profile of v3, /device:TPU:41, one launch (start us, length us, event | category | flops | bytes accessed | tf_op | source)
XLA Modules:
  0.0 76.7 jit_solution(2450778048698086996)
XLA Ops:
  0.0 0.0 copy-start
  0.0 74.1 %attention.1 = (bf16[16,256,256]{2,1,0:T(8,128)(2,1)S(1)}, bf16[16,128,256]{2,1,0:T(8,128)(2,1)S(1)}) custom-call(bf16[256,4096]{1,0:T(8,128)(2,1)} %bitcast.4, bf16[256,512]{1,0:T(8,128)(2,1)} %bitcast.5, bf16[256,512]{1,0:T(8,128)(2,1)} %bitcast.6, s32[32]{0:T(128)} %lengths_hbm.1, s32[256,256]{1,0:T(8,128)} %mask_hbm.1), custom_call_target="tpu_custom_call" | custom-call | tf_op jit(solution)/shard_map/attention/pallas_call | solution.py:431
  74.1 0.0 copy-done
  74.1 2.6 %place.1 = bf16[384,4096]{1,0:T(8,128)(2,1)} custom-call(s32[256]{0:T(256)S(1)} %copy-done, bf16[16,256,256]{2,1,0:T(8,128)(2,1)S(1)} %get-tuple-element.7.own, bf16[16,128,256]{2,1,0:T(8,128)(2,1)S(1)} %get-tuple-element.8.side), custom_call_target="tpu_custom_call" | custom-call | tf_op jit(solution)/shard_map/place/pallas_call | solution.py:459
Async XLA Ops:
  0.0 74.1 %copy-start = (s32[256]{0:T(256)S(1)}, s32[256]{0:T(256)}, u32[]{:S(2)}) copy-start(s32[256]{0:T(256)} %plan.1) | copy-start | bytes 3076

commit v4 on v3

--- a/solution.py
+++ b/solution.py
@@ -190,10 +190,10 @@
                 pl.when(z < d)(lambda: arrive_over(now - d - 1, d))
             if 0 <= now - d < HEADS_KV:
                 pl.when(z >= d)(lambda: arrive(now - d, d))
+        if 0 < now < HEADS_KV:
+            own(now)
         if now < HEADS_KV:
             ready(now, 0)
-        if now + 1 < HEADS_KV:
-            own(now + 1)
         for n in range(HEADS_KV):
             if now == n + 2:
                 at_z(3, stride_one(n).wait_recv, stride_two(n, 2).start)

time: 76.8 us -> 73.7 us (0.960)
  the two profiles are of different devices: /device:TPU:41 before, /device:TPU:1 now
where the time goes in v4:
time: 73.7 us; the launch traced here: 73.6 us
  Pallas kernels  73.6 us (100%)
    pallas_call x1, Pallas kernels, body(): pl.pallas_call(attention_kernel, out_shape=(jax.ShapeDtypeStruct((STEPS,...  70.9 us
    pallas_call x1, Pallas kernels, body(): pl.pallas_call(place_kernel, out_shape=jax.ShapeDtypeStruct((3 * BLOCK, W...  2.63 us

profile of v4, /device:TPU:1, one launch (start us, length us, event | category | flops | bytes accessed | tf_op | source)
XLA Modules:
  0.0 73.6 jit_solution(799436420219452792)
XLA Ops:
  0.0 0.0 copy-start
  0.0 70.9 %attention.1 = (bf16[16,256,256]{2,1,0:T(8,128)(2,1)S(1)}, bf16[16,128,256]{2,1,0:T(8,128)(2,1)S(1)}) custom-call(bf16[256,4096]{1,0:T(8,128)(2,1)} %bitcast.4, bf16[256,512]{1,0:T(8,128)(2,1)} %bitcast.5, bf16[256,512]{1,0:T(8,128)(2,1)} %bitcast.6, s32[32]{0:T(128)} %lengths_hbm.1, s32[256,256]{1,0:T(8,128)} %mask_hbm.1), custom_call_target="tpu_custom_call" | custom-call | tf_op jit(solution)/shard_map/attention/pallas_call | solution.py:431
  70.9 0.0 copy-done
  71.0 2.6 %place.1 = bf16[384,4096]{1,0:T(8,128)(2,1)} custom-call(s32[256]{0:T(256)S(1)} %copy-done, bf16[16,256,256]{2,1,0:T(8,128)(2,1)S(1)} %get-tuple-element.7.own, bf16[16,128,256]{2,1,0:T(8,128)(2,1)S(1)} %get-tuple-element.8.side), custom_call_target="tpu_custom_call" | custom-call | tf_op jit(solution)/shard_map/place/pallas_call | solution.py:459
Async XLA Ops:
  0.0 70.9 %copy-start = (s32[256]{0:T(256)S(1)}, s32[256]{0:T(256)}, u32[]{:S(2)}) copy-start(s32[256]{0:T(256)} %plan.1) | copy-start | bytes 3076
